TPU v7x, 32 devices: a whole 2x2x4 slice. The times are simulated.
32 devices in a mesh: ctx: 2 (over x), ep: 16 (over z, y, core).
Axes of the slice: x: 2, y: 2, z: 4, core: 2. Of those that a mesh axis runs over, the one named last changes fastest.
Arguments:
- moe_rows: bfloat16 [4096, 2048], P(('ctx', 'ep')), may hold values from -6 to 6
- expert_ids: int32 [4096, 8], P(('ctx', 'ep')), may hold values from 0 to 31, all different within a row; in each aligned block of 128 rows (0 to 127, 128 to 255, ...) at most 36 rows name the same one
- expert_gates: bfloat16 [4096, 8], P(('ctx', 'ep')), may hold values from 0.049804688 to 1
- expert_weights: bfloat16 [32, 2048, 1536], P('ep', 'ctx'), may hold values from -0.125 to 0.125
Outputs:
- expert_hidden: bfloat16 [2, 32, 16, 36, 768], P('ctx', 'ep')
Inputs may be any that keep to these rules, and one draw needn't show every extreme that they name: `expert_ids`: each token names 8 different experts; in each aligned block of 128 tokens (the tokens of one device) no expert is named more than 36 times, a bound that some block reaches.
All inputs are finite; a program needn't handle non-finite values.
Results may differ from a plain program's by a relative error of at most 0.0012.
Values may be sent and summed in bfloat16 or wider, within the bound.
A program may use at most 128 MiB of HBM per device.

v0:
```python
import jax
import jax.numpy as jnp
from jax import lax
from jax.sharding import PartitionSpec as P

FF = 768
TOP = 8


def place_rows(block_rows, block_ids, block_gates, experts, capacity):
    flat_ids = block_ids.reshape(-1)
    markers = (flat_ids[:, None] == jnp.arange(experts, dtype=jnp.int32)[None, :]).astype(jnp.int32)
    ranking = jnp.cumsum(markers, axis=0) - markers
    slot_index = jnp.sum(ranking * markers, axis=1)
    places = flat_ids * capacity + slot_index
    owners = jnp.arange(flat_ids.shape[0], dtype=jnp.int32) // block_ids.shape[1]
    buffer = (
        jnp.zeros((experts * capacity, block_rows.shape[1]), block_rows.dtype)
        .at[places]
        .set(block_rows[owners])
    )
    gate_buffer = (
        jnp.zeros((experts * capacity,), block_gates.dtype).at[places].set(block_gates.reshape(-1))
    )
    return (
        buffer.reshape(experts, capacity, block_rows.shape[1]),
        gate_buffer.reshape(experts, capacity),
    )


def project(inputs, weights):
    return jnp.einsum("sucd,udf->uscf", inputs, weights, preferred_element_type=jnp.float32)


def activate(before, gate_values):
    scaled = jnp.transpose(gate_values, (1, 0, 2)).astype(jnp.float32)[..., None]
    return (jax.nn.silu(before[..., :FF]) * before[..., FF:] * scaled).astype(jnp.bfloat16)


def shards(moe_rows, expert_ids, expert_gates, expert_weights):
    sources = lax.axis_size("ep")
    held_experts = expert_weights.shape[0]
    experts = sources * held_experts
    row_count = moe_rows.shape[0]
    capacity = max(2, 9 * row_count * TOP // (8 * experts))
    buffer, gate_buffer = place_rows(moe_rows, expert_ids, expert_gates, experts, capacity)
    buffer = buffer.reshape(sources, held_experts, capacity, buffer.shape[2])
    gate_buffer = gate_buffer.reshape(sources, held_experts, capacity)
    arrived, arrived_gates = (
        lax.all_to_all(buffer, "ep", split_axis=0, concat_axis=0, tiled=True),
        lax.all_to_all(gate_buffer, "ep", split_axis=0, concat_axis=0, tiled=True),
    )
    before = project(arrived, lax.all_gather(expert_weights, "ctx", axis=1, tiled=True))
    hidden = activate(before, arrived_gates)
    return hidden[None]


def solution(mesh):
    in_specs = (
        P(("ctx", "ep"), None),
        P(("ctx", "ep"), None),
        P(("ctx", "ep"), None),
        P("ep", "ctx", None),
    )
    out_specs = P("ctx", "ep", None, None, None)
    return jax.shard_map(shards, mesh=mesh, in_specs=in_specs, out_specs=out_specs, check_vma=False)
```

profile of v0, /device:TPU:15, one launch (start us, length us, event | category | flops | bytes accessed | tf_op | source)
XLA Modules:
  0.0 210.4 jit_solution(10439036497109051874)
XLA Ops:
  6.5 0.7 all-gather.2.cloned.1.call-update
  7.3 0.1 copy.16
  7.4 0.1 eq.29
  7.5 0.1 eq.25
  7.6 9.0 %reduce-window.6 = s32[32,8,128]{2,1,0:T(8,128)S(1)} reduce-window(s32[32,8,128]{2,1,0:T(8,128)S(1)} %fusion.12, s32[]{:T(128)} %constant.28.clone.1), window={size=1x1x128 pad=0_0x0_0x127_0}, to_apply=%region_0.0 | reduce-window | flops 4161536 | bytes 262148 | tf_op jit(solution)/shard_map/reduce-window
  16.6 0.1 slice.18
  16.7 0.1 copy.18
  16.9 0.1 copy.19
  16.9 0.1 copy.15
  17.1 0.1 mul.36
  17.2 0.1 copy.22
  17.3 0.1 reshape.115
  17.4 0.1 broadcast_add_fusion
  17.6 7.6 %scatter_custom_fusion.1 = bf16[1152]{0:T(1024)(128)(2,1)S(1)} fusion(s32[1024]{0:T(1024)S(1)} %bitcast.34, bf16[1024]{0:T(1024)(128)(2,1)S(1)} %reshape.115, bf16[]{:T(256)} %constant.26.clone.1), kind=kCustom, calls=%fused_computation.29 | custom fusion | bytes 2306 | tf_op jit(solution)/shard_map/scatter | solution.py:23
  25.2 0.7 reshape_reshape.7
  25.9 6.6 %all-to-all-start.1 = ((bf16[16,2,36]{2,1,0:T(2,128)(2,1)}), bf16[16,2,36]{2,1,0:T(2,128)(2,1)S(1)}, u32[]{:S(2)}, u32[]{:S(2)}) async-start(bf16[16,2,36]{2,1,0:T(2,128)(2,1)} %reshape_reshape.7), calls=%async_computation.1 | async-start | bytes 16384 | tf_op jit(solution)/shard_map/all_to_all | solution.py:51
  32.5 22.8 %scatter_custom_fusion = bf16[1152,2048]{1,0:T(8,128)(2,1)} fusion(s32[1024]{0:T(1024)S(1)} %bitcast.35, bf16[128,2048]{1,0:T(8,128)(2,1)S(1)} %copy-done, s32[1024]{0:T(1024)S(1)} %broadcast_clamp_fusion, bf16[]{:T(256)} %constant.26.clone.1), kind=kCustom, calls=%fused_computation.6 | custom fusion | bytes 4718594 | tf_op jit(solution)/shard_map/scatter | solution.py:20
  55.3 7.2 %reshape_reshape.6 = bf16[16,2,36,2048]{3,2,1,0:T(8,128)(2,1)} reshape(bf16[1152,2048]{1,0:T(8,128)(2,1)} %scatter_custom_fusion) | data formatting | bytes 9437184 | tf_op jit(solution)/shard_map/reshape;reshape | solution.py:47
  62.5 9.6 %copy.20 = bf16[16,2,36,2048]{3,1,2,0:T(2,128)(2,1)} copy(bf16[16,2,36,2048]{3,2,1,0:T(8,128)(2,1)} %reshape_reshape.6) | data formatting | bytes 9437184 | tf_op jit(solution)/shard_map/reshape;reshape | solution.py:47
  72.1 6.0 %all-to-all-start = ((bf16[16,2,36,2048]{3,1,2,0:T(2,128)(2,1)}), bf16[16,2,36,2048]{3,1,2,0:T(2,128)(2,1)}, u32[]{:S(2)}, u32[]{:S(2)}) async-start(bf16[16,2,36,2048]{3,1,2,0:T(2,128)(2,1)} %copy.20), calls=%async_computation | async-start | bytes 9437184 | tf_op jit(solution)/shard_map/all_to_all | solution.py:50
  78.1 103.7 %all-to-all-done = bf16[16,2,36,2048]{3,1,2,0:T(2,128)(2,1)} async-done(((bf16[16,2,36,2048]{3,1,2,0:T(2,128)(2,1)}), bf16[16,2,36,2048]{3,1,2,0:T(2,128)(2,1)}, u32[]{:S(2)}, u32[]{:S(2)}) %all-to-all-start) | async-done | bytes 4718624 | tf_op jit(solution)/shard_map/all_to_all | solution.py:50
  181.8 19.0 %fusion = f32[2,16,36,1536]{3,2,1,0:T(8,128)S(1)} fusion(bf16[2,2048,1536]{2,1,0:T(8,128)(2,1)} %all-gather.2.cloned.1.call-done, bf16[16,2,36,2048]{3,1,2,0:T(2,128)(2,1)} %all-to-all-done), kind=kOutput, calls=%fused_computation.3 | convolution fusion | flops 7247757312 | bytes 24379392 | tf_op jit(solution)/shard_map/sucd,udf->uscf/dot_general | solution.py:32
  200.9 1.2 fusion.8
  202.0 1.5 copy.24
  (19 shorter events, 0.2 us)
Async XLA Ops:
  6.5 25.9 %copy-start = (bf16[128,2048]{1,0:T(8,128)(2,1)S(1)}, bf16[128,2048]{1,0:T(8,128)(2,1)}, u32[]{:S(2)}) copy-start(bf16[128,2048]{1,0:T(8,128)(2,1)} %param.4) | copy-start | bytes 1572868
  6.5 0.7 copy-start.1
  6.5 10.6 %copy-start.2 = (bf16[128,8]{0,1:T(8,128)(2,1)S(1)}, bf16[128,8]{0,1:T(8,128)(2,1)}, u32[]{:S(2)}) copy-start(bf16[128,8]{0,1:T(8,128)(2,1)} %param.6) | copy-start | bytes 6148
  6.5 175.3 %all-gather.2.cloned.1.call-start = ((), (), s32[]{:S(2)}) async-start(), calls=%async_computation.2 | async-start | bytes 18874368 | tf_op jit(solution)/shard_map/all_gather | solution.py:53
  25.9 46.2 %all-to-all-start.1 = ((bf16[16,2,36]{2,1,0:T(2,128)(2,1)}), bf16[16,2,36]{2,1,0:T(2,128)(2,1)S(1)}, u32[]{:S(2)}, u32[]{:S(2)}) async-start(bf16[16,2,36]{2,1,0:T(2,128)(2,1)} %reshape_reshape.7), calls=%async_computation.1 | async-start | bytes 16384 | tf_op jit(solution)/shard_map/all_to_all | solution.py:51
  72.1 109.7 %all-to-all-start = ((bf16[16,2,36,2048]{3,1,2,0:T(2,128)(2,1)}), bf16[16,2,36,2048]{3,1,2,0:T(2,128)(2,1)}, u32[]{:S(2)}, u32[]{:S(2)}) async-start(bf16[16,2,36,2048]{3,1,2,0:T(2,128)(2,1)} %copy.20), calls=%async_computation | async-start | bytes 9437184 | tf_op jit(solution)/shard_map/all_to_all | solution.py:50
Sparse Core Ops, SparseCore 0:
  8.9 151.7 all-gather.1
where the time goes:
time: 211 us; the launch traced here: 210 us
  waiting for transfers between devices  104 us (49%)
  local copies, waits for them, and re-layouts  50.5 us (24%)
  matrix products  19 us (9%)
  between operations  13.5 us (6%)
  starting transfers between devices  12.6 us (6%)
  other arithmetic  10.4 us (5%)
    all_to_all x1, waiting for transfers between devices, shards(): lax.all_to_all(buffer, 'ep', split_axis=0, concat_axis=0, tiled=True)  104 us
    scatter x1, local copies, waits for them, and re-layouts, place_rows(): buffer = jnp.zeros((experts * capacity, block_rows.shape[1]), block_rows....  22.8 us
    dot_general x1, matrix products, project(): jnp.einsum('sucd,udf->uscf', inputs, weights, preferred_element_type=jnp....  19 us
    another operation x2, local copies, waits for them, and re-layouts, shards(): buffer = buffer.reshape(sources, held_experts, capacity, buffer.shape[2])  16.8 us
    another operation x3, other arithmetic  9.14 us
    scatter x1, local copies, waits for them, and re-layouts, place_rows(): jnp.zeros((experts * capacity,), block_gates.dtype).at[places]  7.59 us
    all_to_all x1, starting transfers between devices, shards(): lax.all_to_all(gate_buffer, 'ep', split_axis=0, concat_axis=0, tiled=True)  6.56 us
    all_to_all x1, starting transfers between devices, shards(): lax.all_to_all(buffer, 'ep', split_axis=0, concat_axis=0, tiled=True)  6.02 us
  transfers between devices with their start and end apart: 3, of which 1 were waited for; matrix products, arithmetic and copies ran while one was open for 28% of the time, Pallas kernels for 0%

commit v1 on v0

--- a/solution.py
+++ b/solution.py
@@ -1,10 +1,20 @@
+import functools
+import math
+
 import jax
 import jax.numpy as jnp
 from jax import lax
+from jax.experimental import pallas as pl
+from jax.experimental.pallas import tpu as pltpu
 from jax.sharding import PartitionSpec as P
 
 FF = 768
 TOP = 8
+ROW_BOUND = 6.0
+WEIGHT_BOUND = 0.125
+META = 16
+ZS = 4
+CHIPS = 8
 
 
 def place_rows(block_rows, block_ids, block_gates, experts, capacity):
@@ -37,7 +47,7 @@
     return (jax.nn.silu(before[..., :FF]) * before[..., FF:] * scaled).astype(jnp.bfloat16)
 
 
-def shards(moe_rows, expert_ids, expert_gates, expert_weights):
+def general_shards(moe_rows, expert_ids, expert_gates, expert_weights):
     sources = lax.axis_size("ep")
     held_experts = expert_weights.shape[0]
     experts = sources * held_experts
@@ -55,6 +65,313 @@
     return hidden[None]
 
 
+def chip_at_step(step, z, y):
+    first, last, odd = (7 - step) // 7, step // 7, step % 2
+    other = (1 - odd) * (1 - first) + last
+    i = odd * ((step + 1) // 2) + (1 - odd) * (step // 2 - 1) + first - last
+    mirror = z // 2
+    inner = mirror * (ZS - 1 - z) + (1 - mirror) * z
+    near = 1 - i // 2
+    w = inner * (near * (1 - i) + (1 - near) * i) + (1 - inner) * i
+    zs = mirror * (ZS - 1 - w) + (1 - mirror) * w
+    ys = y + other * (1 - 2 * y)
+    return zs, ys, other
+
+
+def encode(p, scale):
+    q = p * scale
+    q2 = q * q
+    q4 = q2 * q2
+    q8 = q4 * q4
+    return jnp.where(q < 0, -q8, q8).astype(jnp.bfloat16)
+
+
+def decode(code, scale):
+    v = code.astype(jnp.float32)
+    size = jnp.exp(jnp.log(jnp.abs(v)) * 0.125) * (1.0 / scale)
+    return jnp.where(v < 0, -size, size)
+
+
+def kernel(
+    cap, scale,
+    rows_ref, ids_ref, gates_ref, weights_hbm, out_ref,
+    blocks, weights, mine, sent, got, gate_rows,
+    load_sem, weight_sem, x_send, x_recv, up_send, down_send, y_send, core_send, unit_recv,
+    part_send, part_recv,
+):
+    tokens, width = rows_ref.shape
+    half = width // 2
+    held = weights_hbm.shape[0]
+    c = lax.axis_index("ctx")
+    e = lax.axis_index("ep")
+    z, y, k = e // 4, (e // 2) % 2, e % 2
+    chip = 2 * z + y
+    x_peer = {"ctx": 1 - c, "ep": e}
+    y_peer = {"ctx": c, "ep": 4 * z + 2 * (1 - y) + k}
+    core_peer = {"ctx": c, "ep": 4 * z + 2 * y + 1 - k}
+    up_peer = {"ctx": c, "ep": e + 4}
+    down_peer = {"ctx": c, "ep": e - 4}
+    not_top, not_bottom = z < ZS - 1, z > 0
+
+    barrier = pltpu.get_barrier_semaphore()
+
+    def greet(peer):
+        pl.semaphore_signal(barrier, inc=1, device_id=peer, device_id_type=pl.DeviceIdType.MESH)
+
+    greet(x_peer)
+    greet(y_peer)
+    greet(core_peer)
+
+    @pl.when(not_top)
+    def _():
+        greet(up_peer)
+
+    @pl.when(not_bottom)
+    def _():
+        greet(down_peer)
+
+    load = pltpu.make_async_copy(
+        rows_ref.at[:, pl.ds(pl.multiple_of(c * half, half), half)],
+        blocks.at[chip, k, c, pl.ds(0, tokens)],
+        load_sem,
+    )
+    load.start()
+    weight_loads = [
+        pltpu.make_async_copy(weights_hbm.at[j], weights.at[j], weight_sem.at[j]) for j in range(held)
+    ]
+    for w in weight_loads:
+        w.start()
+
+    lane = lax.broadcasted_iota(jnp.int32, (tokens, 128), 1)
+    ids = ids_ref[...]
+    gates = gates_ref[...].astype(jnp.float32)
+    marks = jnp.zeros((tokens, 128), jnp.float32)
+    gate_of = jnp.zeros((tokens, 128), jnp.float32)
+    for t in range(TOP):
+        same = ids[:, t : t + 1] == lane
+        marks = marks + jnp.where(same, 1.0, 0.0)
+        gate_of = gate_of + jnp.where(same, gates[:, t : t + 1], 0.0)
+    marks, gate_of = marks.T[:32], gate_of.T[:32]
+    earlier = (
+        lax.broadcasted_iota(jnp.int32, (tokens, tokens), 0)
+        < lax.broadcasted_iota(jnp.int32, (tokens, tokens), 1)
+    )
+    rank = jnp.dot(
+        marks.astype(jnp.bfloat16),
+        jnp.where(earlier, 1.0, 0.0).astype(jnp.bfloat16),
+        preferred_element_type=jnp.float32,
+    )
+    slots = jnp.where(marks > 0, rank, -1.0)
+    table = jnp.concatenate(
+        [slots[:16], slots[16:], gate_of[:16], gate_of[16:], jnp.zeros((META, half - 512), jnp.float32)],
+        axis=1,
+    )
+    blocks[chip, k, c, tokens:, :] = table.astype(jnp.bfloat16)
+
+    pl.semaphore_wait(barrier, 3 + (z + ZS - 1) // ZS + (2 * ZS - 2 - z) // ZS)
+
+    def remote(src, dst, send_sem, recv_sem, peer):
+        return pltpu.make_async_remote_copy(
+            src_ref=src, dst_ref=dst, send_sem=send_sem, recv_sem=recv_sem,
+            device_id=peer, device_id_type=pl.DeviceIdType.MESH,
+        )
+
+    def x_rows(plane):
+        return remote(
+            rows_ref.at[:, pl.ds(pl.multiple_of((1 - c) * half, half), half)],
+            blocks.at[chip, k, plane, pl.ds(0, tokens)],
+            x_send.at[0], x_recv.at[0], x_peer,
+        )
+
+    def x_table(plane):
+        return remote(
+            blocks.at[chip, k, plane, pl.ds(tokens, META)],
+            blocks.at[chip, k, plane, pl.ds(tokens, META)],
+            x_send.at[1], x_recv.at[1], x_peer,
+        )
+
+    x_rows(c).start()
+    x_table(c).start()
+    load.wait()
+
+    def unit_copy(g, core, plane, send_sem, peer):
+        unit = blocks.at[g, core, plane]
+        return remote(unit, unit, send_sem, unit_recv.at[(g * 2 + core) * 2 + plane], peer)
+
+    def each_send(step, plane, act):
+        zs, ys, other = chip_at_step(step, z, y)
+        g = 2 * zs + ys
+
+        @pl.when((other == 0) & not_top & (zs <= z))
+        def _():
+            act(unit_copy(g, k, plane, up_send.at[zs * 2 + plane], up_peer))
+
+        @pl.when((other == 0) & not_bottom & (zs >= z))
+        def _():
+            act(unit_copy(g, k, plane, down_send.at[zs * 2 + plane], down_peer))
+
+        @pl.when(other == 0)
+        def _():
+            act(unit_copy(g, k, plane, y_send.at[zs * 2 + plane], y_peer))
+
+        act(unit_copy(g, k, plane, core_send.at[g * 2 + plane], core_peer))
+
+    def part_copy(g):
+        return remote(sent.at[g], got.at[g], part_send.at[g], part_recv.at[g], x_peer)
+
+    def compute(g):
+        units = [(0, 1 - c), (1, 1 - c), (0, c), (1, c)]
+        x = jnp.concatenate([blocks[g, core, plane, :tokens, :] for core, plane in units], axis=0)
+        pick = lax.broadcasted_iota(jnp.int32, (META, 128), 0)
+        at = pl.multiple_of((e // 8) * 128, 128)
+        slot_tables = [
+            blocks[g, core, plane, tokens:, pl.ds(at, 128)].astype(jnp.float32) for core, plane in units
+        ]
+        gate_at = pl.multiple_of((e // 8) * 128 + 256, 128)
+        gate_tables = [
+            blocks[g, core, plane, tokens:, pl.ds(gate_at, 128)].astype(jnp.float32)
+            for core, plane in units[2:]
+        ]
+        target = lax.broadcasted_iota(jnp.int32, (4 * cap, 4 * tokens), 0).astype(jnp.float32)
+        chosen, gate_columns = [], []
+        for j in range(held):
+            here = pick == (e % 8) * 2 + j
+            places = []
+            for u, slot_table in enumerate(slot_tables):
+                slot = jnp.sum(jnp.where(here, slot_table, 0.0), axis=0, keepdims=True)
+                places.append(jnp.where(slot >= 0, slot + float(u * cap), -1.0))
+            hot = target == jnp.concatenate(places, axis=1)
+            gate_line = jnp.concatenate(
+                [jnp.sum(jnp.where(here, t, 0.0), axis=0, keepdims=True) for t in gate_tables], axis=1
+            )
+            gate_columns.append(
+                jnp.sum(
+                    jnp.where(hot[2 * cap :, 2 * tokens :], gate_line, 0.0), axis=1, keepdims=True
+                )
+            )
+            chosen.append(
+                jnp.dot(
+                    jnp.where(hot, 1.0, 0.0).astype(jnp.bfloat16), x, preferred_element_type=jnp.float32
+                ).astype(jnp.bfloat16)
+            )
+        gate_rows[g] = jnp.broadcast_to(jnp.concatenate(gate_columns, axis=0), (held * 2 * cap, 128))
+        step = 512
+        for n in range(0, 2 * FF, step):
+            parts = [
+                jnp.dot(chosen[j], weights[j, :, n : n + step], preferred_element_type=jnp.float32)
+                for j in range(held)
+            ]
+            sent[g, :, n : n + step] = encode(
+                jnp.concatenate([p[: 2 * cap] for p in parts], axis=0), scale
+            )
+            mine[g, :, n : n + step] = jnp.concatenate([p[2 * cap :] for p in parts], axis=0)
+
+    def work(step, carry):
+        zs, ys, other = chip_at_step(step, z, y)
+        g = 2 * zs + ys
+        for i in range(2):
+            plane = c if i == 0 else 1 - c
+
+            @pl.when(step > 0)
+            def _():
+                unit_copy(g, k, plane, core_send.at[g * 2 + plane], core_peer).wait_recv()
+
+            if i == 1:
+
+                @pl.when(step == 0)
+                def _():
+                    x_rows(plane).wait_recv()
+                    x_table(plane).wait_recv()
+
+            each_send(step, plane, lambda copy: copy.start())
+        for i in range(2):
+            plane = c if i == 0 else 1 - c
+            unit_copy(g, 1 - k, plane, core_send.at[g * 2 + plane], core_peer).wait_recv()
+
+        @pl.when(step == 0)
+        def _():
+            for w in weight_loads:
+                w.wait()
+
+        compute(g)
+        part_copy(g).start()
+        return carry
+
+    lax.fori_loop(0, CHIPS, work, 0)
+
+    def finish(step, carry):
+        zs, ys, _ = chip_at_step(step, z, y)
+        g = 2 * zs + ys
+        part_copy(g).wait_recv()
+        gate_column = gate_rows[g, :, 0:1]
+        first = mine[g, :, :FF] + decode(got[g, :, :FF], scale)
+        second = mine[g, :, FF:] + decode(got[g, :, FF:], scale)
+        hidden = first / (1.0 + jnp.exp(-first)) * second * gate_column
+        for j in range(held):
+            for core in range(2):
+                low = (j * 2 + core) * cap
+                out_ref[0, j, 2 * g + core] = hidden[low : low + cap].astype(jnp.bfloat16)
+        return carry
+
+    lax.fori_loop(0, CHIPS, finish, 0)
+
+    def drain(step, carry):
+        zs, ys, _ = chip_at_step(step, z, y)
+        for plane in (c, 1 - c):
+            each_send(step, plane, lambda copy: copy.wait_send())
+        part_copy(2 * zs + ys).wait_send()
+        return carry
+
+    lax.fori_loop(0, CHIPS, drain, 0)
+    x_rows(c).wait_send()
+    x_table(c).wait_send()
+
+
+def kernel_shards(moe_rows, expert_ids, expert_gates, expert_weights):
+    sources = lax.axis_size("ep")
+    tokens, width = moe_rows.shape
+    held, half, columns = expert_weights.shape
+    cap = max(2, 9 * tokens * TOP // (8 * sources * held))
+    part_rows = held * 2 * cap
+    scale = 2.0 ** math.floor(math.log2(49152.0 / (half * ROW_BOUND * WEIGHT_BOUND)))
+    dma = pltpu.SemaphoreType.DMA
+    vmem = pl.BlockSpec(memory_space=pltpu.VMEM)
+    hbm = pl.BlockSpec(memory_space=pl.ANY)
+    return pl.pallas_call(
+        functools.partial(kernel, cap, scale),
+        out_shape=jax.ShapeDtypeStruct((1, held, sources, cap, columns // 2), jnp.bfloat16),
+        in_specs=[hbm, vmem, vmem, hbm],
+        out_specs=vmem,
+        scratch_shapes=[
+            pltpu.VMEM((CHIPS, 2, 2, tokens + META, half), jnp.bfloat16),
+            pltpu.VMEM((held, half, columns), jnp.bfloat16),
+            pltpu.VMEM((CHIPS, part_rows, columns), jnp.float32),
+            pltpu.VMEM((CHIPS, part_rows, columns), jnp.bfloat16),
+            pltpu.VMEM((CHIPS, part_rows, columns), jnp.bfloat16),
+            pltpu.VMEM((CHIPS, part_rows, 128), jnp.float32),
+            dma,
+            dma((held,)),
+            dma((2,)),
+            dma((2,)),
+            dma((2 * ZS,)),
+            dma((2 * ZS,)),
+            dma((2 * ZS,)),
+            dma((2 * CHIPS,)),
+            dma((4 * CHIPS,)),
+            dma((CHIPS,)),
+            dma((CHIPS,)),
+        ],
+        compiler_params=pltpu.CompilerParams(
+            collective_id=0, has_side_effects=True, vmem_limit_bytes=56 * 1024 * 1024
+        ),
+        cost_estimate=pl.CostEstimate(
+            flops=2 * CHIPS * held * 4 * cap * half * columns,
+            bytes_accessed=held * half * columns * 2,
+            transcendentals=0,
+        ),
+    )(moe_rows, expert_ids, expert_gates, expert_weights)
+
+
 def solution(mesh):
     in_specs = (
         P(("ctx", "ep"), None),
@@ -63,4 +380,6 @@
         P("ep", "ctx", None),
     )
     out_specs = P("ctx", "ep", None, None, None)
-    return jax.shard_map(shards, mesh=mesh, in_specs=in_specs, out_specs=out_specs, check_vma=False)
+    fits = mesh.shape["ctx"] == 2 and mesh.shape["ep"] == 2 * CHIPS
+    body = kernel_shards if fits else general_shards
+    return jax.shard_map(body, mesh=mesh, in_specs=in_specs, out_specs=out_specs, check_vma=False)

time: 211 us -> 101 us (0.48)
  the two profiles are of different devices: /device:TPU:15 before, /device:TPU:0 now
where the time goes in v1:
time: 101 us; the launch traced here: 100 us
  Pallas kernels  94.5 us (94%)
  local copies, waits for them, and re-layouts  5.88 us (6%)
    pallas_call x1, Pallas kernels, kernel_shards(): pl.pallas_call(functools.partial(kernel, cap, scale), out_shape=jax.Shape...  94.5 us
    pallas_call x1, local copies, waits for them, and re-layouts, kernel_shards(): pl.pallas_call(functools.partial(kernel, cap, scale), out_shape=jax.Shape...  3.08 us
    unnamed x2, local copies, waits for them, and re-layouts  2.8 us

profile of v1, /device:TPU:0, one launch (start us, length us, event | category | flops | bytes accessed | tf_op | source)
XLA Modules:
  0.0 100.4 jit_solution(4514522039414461744)
XLA Ops:
  0.0 1.4 %copy.6.gates_ref = bf16[128,8]{1,0:T(8,128)(2,1)} copy(bf16[128,8]{0,1:T(8,128)(2,1)} %param.6) | data formatting | bytes 4096 | tf_op args[2]
  1.4 1.4 %copy.5.ids_ref = s32[128,8]{1,0:T(8,128)} copy(s32[128,8]{0,1:T(8,128)} %param.5) | data formatting | bytes 8192 | tf_op args[1]
  2.8 94.5 %shard_map.46 = bf16[1,2,16,36,768]{4,3,2,1,0:T(8,128)(2,1)} custom-call(bf16[128,2048]{1,0:T(8,128)(2,1)} %rows_ref.1, s32[128,8]{1,0:T(8,128)} %copy.5.ids_ref, bf16[128,8]{1,0:T(8,128)(2,1)} %copy.6.gates_ref, bf16[2,1024,1536]{2,1,0:T(8,128)(2,1)} %weights_hbm.1), custom_call_target="tpu_custom_call" | custom-call | flops 7247757312 | bytes 6291456 | tf_op jit(solution)/shard_map/pallas_call | solution.py:340
  97.3 3.1 %copy.7 = bf16[1,2,16,36,768]{4,2,3,1,0:T(8,128)(2,1)} copy(bf16[1,2,16,36,768]{4,3,2,1,0:T(8,128)(2,1)} %shard_map.46) | data formatting | bytes 3538944 | tf_op jit(solution)/shard_map/pallas_call | solution.py:340

commit v2 on v1

--- a/solution.py
+++ b/solution.py
@@ -15,6 +15,7 @@
 META = 16
 ZS = 4
 CHIPS = 8
+CHUNKS = 3
 
 
 def place_rows(block_rows, block_ids, block_gates, experts, capacity):
@@ -102,6 +103,7 @@
     tokens, width = rows_ref.shape
     half = width // 2
     held = weights_hbm.shape[0]
+    chunk = FF // CHUNKS
     c = lax.axis_index("ctx")
     e = lax.axis_index("ep")
     z, y, k = e // 4, (e // 2) % 2, e % 2
@@ -142,16 +144,15 @@
     for w in weight_loads:
         w.start()
 
-    lane = lax.broadcasted_iota(jnp.int32, (tokens, 128), 1)
+    expert = lax.broadcasted_iota(jnp.int32, (32, tokens), 0)
     ids = ids_ref[...]
     gates = gates_ref[...].astype(jnp.float32)
-    marks = jnp.zeros((tokens, 128), jnp.float32)
-    gate_of = jnp.zeros((tokens, 128), jnp.float32)
+    marks = jnp.zeros((32, tokens), jnp.float32)
+    gate_of = jnp.zeros((32, tokens), jnp.float32)
     for t in range(TOP):
-        same = ids[:, t : t + 1] == lane
+        same = ids[t : t + 1] == expert
         marks = marks + jnp.where(same, 1.0, 0.0)
-        gate_of = gate_of + jnp.where(same, gates[:, t : t + 1], 0.0)
-    marks, gate_of = marks.T[:32], gate_of.T[:32]
+        gate_of = gate_of + jnp.where(same, gates[t : t + 1], 0.0)
     earlier = (
         lax.broadcasted_iota(jnp.int32, (tokens, tokens), 0)
         < lax.broadcasted_iota(jnp.int32, (tokens, tokens), 1)
@@ -202,6 +203,8 @@
         zs, ys, other = chip_at_step(step, z, y)
         g = 2 * zs + ys
 
+        act(unit_copy(g, k, plane, core_send.at[g * 2 + plane], core_peer))
+
         @pl.when((other == 0) & not_top & (zs <= z))
         def _():
             act(unit_copy(g, k, plane, up_send.at[zs * 2 + plane], up_peer))
@@ -214,10 +217,9 @@
         def _():
             act(unit_copy(g, k, plane, y_send.at[zs * 2 + plane], y_peer))
 
-        act(unit_copy(g, k, plane, core_send.at[g * 2 + plane], core_peer))
-
-    def part_copy(g):
-        return remote(sent.at[g], got.at[g], part_send.at[g], part_recv.at[g], x_peer)
+    def part_copy(g, n):
+        at = g * CHUNKS + n
+        return remote(sent.at[g, n], got.at[g, n], part_send.at[at], part_recv.at[at], x_peer)
 
     def compute(g):
         units = [(0, 1 - c), (1, 1 - c), (0, c), (1, c)]
@@ -255,16 +257,19 @@
                 ).astype(jnp.bfloat16)
             )
         gate_rows[g] = jnp.broadcast_to(jnp.concatenate(gate_columns, axis=0), (held * 2 * cap, 128))
-        step = 512
-        for n in range(0, 2 * FF, step):
-            parts = [
-                jnp.dot(chosen[j], weights[j, :, n : n + step], preferred_element_type=jnp.float32)
-                for j in range(held)
-            ]
-            sent[g, :, n : n + step] = encode(
-                jnp.concatenate([p[: 2 * cap] for p in parts], axis=0), scale
-            )
-            mine[g, :, n : n + step] = jnp.concatenate([p[2 * cap :] for p in parts], axis=0)
+        for n in range(CHUNKS):
+            for side in range(2):
+                columns = slice(side * FF + n * chunk, side * FF + (n + 1) * chunk)
+                parts = [
+                    jnp.dot(chosen[j], weights[j, :, columns], preferred_element_type=jnp.float32)
+                    for j in range(held)
+                ]
+                here = slice(side * chunk, (side + 1) * chunk)
+                sent[g, n, :, here] = encode(
+                    jnp.concatenate([p[: 2 * cap] for p in parts], axis=0), scale
+                )
+                mine[g, n, :, here] = jnp.concatenate([p[2 * cap :] for p in parts], axis=0)
+            part_copy(g, n).start()
 
     def work(step, carry):
         zs, ys, other = chip_at_step(step, z, y)
@@ -294,7 +299,6 @@
                 w.wait()
 
         compute(g)
-        part_copy(g).start()
         return carry
 
     lax.fori_loop(0, CHIPS, work, 0)
@@ -302,15 +306,18 @@
     def finish(step, carry):
         zs, ys, _ = chip_at_step(step, z, y)
         g = 2 * zs + ys
-        part_copy(g).wait_recv()
         gate_column = gate_rows[g, :, 0:1]
-        first = mine[g, :, :FF] + decode(got[g, :, :FF], scale)
-        second = mine[g, :, FF:] + decode(got[g, :, FF:], scale)
-        hidden = first / (1.0 + jnp.exp(-first)) * second * gate_column
-        for j in range(held):
-            for core in range(2):
-                low = (j * 2 + core) * cap
-                out_ref[0, j, 2 * g + core] = hidden[low : low + cap].astype(jnp.bfloat16)
+        for n in range(CHUNKS):
+            part_copy(g, n).wait_recv()
+            first = mine[g, n, :, :chunk] + decode(got[g, n, :, :chunk], scale)
+            second = mine[g, n, :, chunk:] + decode(got[g, n, :, chunk:], scale)
+            hidden = first / (1.0 + jnp.exp(-first)) * second * gate_column
+            for j in range(held):
+                for core in range(2):
+                    low = (j * 2 + core) * cap
+                    out_ref[0, j, 2 * g + core, :, n * chunk : (n + 1) * chunk] = hidden[
+                        low : low + cap
+                    ].astype(jnp.bfloat16)
         return carry
 
     lax.fori_loop(0, CHIPS, finish, 0)
@@ -319,7 +326,8 @@
         zs, ys, _ = chip_at_step(step, z, y)
         for plane in (c, 1 - c):
             each_send(step, plane, lambda copy: copy.wait_send())
-        part_copy(2 * zs + ys).wait_send()
+        for n in range(CHUNKS):
+            part_copy(2 * zs + ys, n).wait_send()
         return carry
 
     lax.fori_loop(0, CHIPS, drain, 0)
@@ -339,15 +347,15 @@
     hbm = pl.BlockSpec(memory_space=pl.ANY)
     return pl.pallas_call(
         functools.partial(kernel, cap, scale),
-        out_shape=jax.ShapeDtypeStruct((1, held, sources, cap, columns // 2), jnp.bfloat16),
+        out_shape=pltpu.VMEM((1, held, sources, cap, columns // 2), jnp.bfloat16),
         in_specs=[hbm, vmem, vmem, hbm],
         out_specs=vmem,
         scratch_shapes=[
             pltpu.VMEM((CHIPS, 2, 2, tokens + META, half), jnp.bfloat16),
             pltpu.VMEM((held, half, columns), jnp.bfloat16),
-            pltpu.VMEM((CHIPS, part_rows, columns), jnp.float32),
-            pltpu.VMEM((CHIPS, part_rows, columns), jnp.bfloat16),
-            pltpu.VMEM((CHIPS, part_rows, columns), jnp.bfloat16),
+            pltpu.VMEM((CHIPS, CHUNKS, part_rows, columns // CHUNKS), jnp.float32),
+            pltpu.VMEM((CHIPS, CHUNKS, part_rows, columns // CHUNKS), jnp.bfloat16),
+            pltpu.VMEM((CHIPS, CHUNKS, part_rows, columns // CHUNKS), jnp.bfloat16),
             pltpu.VMEM((CHIPS, part_rows, 128), jnp.float32),
             dma,
             dma((held,)),
@@ -358,8 +366,8 @@
             dma((2 * ZS,)),
             dma((2 * CHIPS,)),
             dma((4 * CHIPS,)),
-            dma((CHIPS,)),
-            dma((CHIPS,)),
+            dma((CHIPS * CHUNKS,)),
+            dma((CHIPS * CHUNKS,)),
         ],
         compiler_params=pltpu.CompilerParams(
             collective_id=0, has_side_effects=True, vmem_limit_bytes=56 * 1024 * 1024
@@ -369,7 +377,7 @@
             bytes_accessed=held * half * columns * 2,
             transcendentals=0,
         ),
-    )(moe_rows, expert_ids, expert_gates, expert_weights)
+    )(moe_rows, expert_ids.T, expert_gates.T, expert_weights)
 
 
 def solution(mesh):

time: 101 us -> 94 us (0.931)
  local copies, waits for them, and re-layouts: 5.88 us -> 1.53 us
  Pallas kernels: 94.5 us -> 92.2 us
    unnamed x2 -> x0, local copies, waits for them, and re-layouts: 2.8 us -> none
    pallas_call x1, Pallas kernels: 94.5 us -> 92.2 us  [kernel_shards(): pl.pallas_call(functools.partial(kernel, cap, scale), out_shape=pltpu.VME...]
    pallas_call x1, local copies, waits for them, and re-layouts: 3.08 us -> 1.53 us  [kernel_shards(): pl.pallas_call(functools.partial(kernel, cap, scale), out_shape=pltpu.VME...]
where the time goes in v2:
time: 94 us; the launch traced here: 93.8 us
  Pallas kernels  92.2 us (98%)
  local copies, waits for them, and re-layouts  1.53 us (2%)
    pallas_call x1, Pallas kernels, kernel_shards(): pl.pallas_call(functools.partial(kernel, cap, scale), out_shape=pltpu.VME...  92.2 us

profile of v2, /device:TPU:0, one launch (start us, length us, event | category | flops | bytes accessed | tf_op | source)
XLA Modules:
  0.0 93.8 jit_solution(15413209447486398263)
XLA Ops:
  0.0 92.2 %shard_map.46 = bf16[1,2,16,36,768]{4,3,2,1,0:T(8,128)(2,1)S(1)} custom-call(bf16[128,2048]{1,0:T(8,128)(2,1)} %rows_ref.1, s32[8,128]{1,0:T(8,128)} %bitcast.2, bf16[8,128]{1,0:T(8,128)(2,1)} %bitcast.3, bf16[2,1024,1536]{2,1,0:T(8,128)(2,1)} %weights_hbm.1), custom_call_target="tpu_custom_call" | custom-call | flops 7247757312 | bytes 6291456 | tf_op jit(solution)/shard_map/pallas_call | solution.py:348
  92.2 1.5 %copy.5 = bf16[1,2,16,36,768]{4,2,3,1,0:T(8,128)(2,1)} copy(bf16[1,2,16,36,768]{4,3,2,1,0:T(8,128)(2,1)S(1)} %shard_map.46) | data formatting | bytes 3538944 | tf_op jit(solution)/shard_map/pallas_call | solution.py:348

commit v3 on v2

--- a/solution.py
+++ b/solution.py
@@ -15,7 +15,7 @@
 META = 16
 ZS = 4
 CHIPS = 8
-CHUNKS = 3
+CHUNKS = 6
 
 
 def place_rows(block_rows, block_ids, block_gates, experts, capacity):
@@ -139,7 +139,14 @@
     )
     load.start()
     weight_loads = [
-        pltpu.make_async_copy(weights_hbm.at[j], weights.at[j], weight_sem.at[j]) for j in range(held)
+        pltpu.make_async_copy(
+            weights_hbm.at[j, :, pl.ds(side * FF + n * chunk, chunk)],
+            weights.at[n, j, :, pl.ds(side * chunk, chunk)],
+            weight_sem.at[(n * held + j) * 2 + side],
+        )
+        for n in range(CHUNKS)
+        for j in range(held)
+        for side in range(2)
     ]
     for w in weight_loads:
         w.start()
@@ -168,6 +175,7 @@
         axis=1,
     )
     blocks[chip, k, c, tokens:, :] = table.astype(jnp.bfloat16)
+    blocks[chip, k, 1 - c, tokens:, 512:] = jnp.zeros((META, half - 512), jnp.bfloat16)
 
     pl.semaphore_wait(barrier, 3 + (z + ZS - 1) // ZS + (2 * ZS - 2 - z) // ZS)
 
@@ -186,8 +194,8 @@
 
     def x_table(plane):
         return remote(
-            blocks.at[chip, k, plane, pl.ds(tokens, META)],
-            blocks.at[chip, k, plane, pl.ds(tokens, META)],
+            blocks.at[chip, k, plane, pl.ds(tokens, META), pl.ds(0, 512)],
+            blocks.at[chip, k, plane, pl.ds(tokens, META), pl.ds(0, 512)],
             x_send.at[1], x_recv.at[1], x_peer,
         )
 
@@ -221,84 +229,82 @@
         at = g * CHUNKS + n
         return remote(sent.at[g, n], got.at[g, n], part_send.at[at], part_recv.at[at], x_peer)
 
-    def compute(g):
-        units = [(0, 1 - c), (1, 1 - c), (0, c), (1, c)]
-        x = jnp.concatenate([blocks[g, core, plane, :tokens, :] for core, plane in units], axis=0)
+    def place(g, plane, gates_too):
+        x = jnp.concatenate([blocks[g, core, plane, :tokens, :] for core in range(2)], axis=0)
         pick = lax.broadcasted_iota(jnp.int32, (META, 128), 0)
-        at = pl.multiple_of((e // 8) * 128, 128)
-        slot_tables = [
-            blocks[g, core, plane, tokens:, pl.ds(at, 128)].astype(jnp.float32) for core, plane in units
+        row = lax.broadcasted_iota(jnp.int32, (2 * cap, 2 * tokens), 0).astype(jnp.float32)
+
+        def lines(first, j):
+            at = pl.multiple_of((e // 8) * 128 + first, 128)
+            return [
+                jnp.sum(
+                    jnp.where(
+                        pick == (e % 8) * 2 + j,
+                        blocks[g, core, plane, tokens:, pl.ds(at, 128)].astype(jnp.float32),
+                        0.0,
+                    ),
+                    axis=0,
+                    keepdims=True,
+                )
+                for core in range(2)
+            ]
+
+        hots, gate_columns = [], []
+        for j in range(held):
+            near, far = lines(0, j)
+            far = jnp.where(far >= 0, far + float(cap), -1.0)
+            hot = row == jnp.concatenate([near, far], axis=1)
+            hots.append(jnp.where(hot, 1.0, 0.0))
+            if gates_too:
+                gate_line = jnp.concatenate(lines(256, j), axis=1)
+                gate_columns.append(jnp.sum(jnp.where(hot, gate_line, 0.0), axis=1, keepdims=True))
+        if gates_too:
+            column = jnp.concatenate(gate_columns, axis=0)
+            gate_rows[g] = jnp.broadcast_to(column, (held * 2 * cap, 128))
+        return jnp.dot(
+            jnp.concatenate(hots, axis=0).astype(jnp.bfloat16), x, preferred_element_type=jnp.float32
+        )
+
+    def compute(g, theirs, ours):
+        rows = [slice(j * 2 * cap, (j + 1) * 2 * cap) for j in range(held)]
+        chosen = [
+            jnp.concatenate([theirs[r], ours[r]], axis=0).astype(jnp.bfloat16) for r in rows
         ]
-        gate_at = pl.multiple_of((e // 8) * 128 + 256, 128)
-        gate_tables = [
-            blocks[g, core, plane, tokens:, pl.ds(gate_at, 128)].astype(jnp.float32)
-            for core, plane in units[2:]
-        ]
-        target = lax.broadcasted_iota(jnp.int32, (4 * cap, 4 * tokens), 0).astype(jnp.float32)
-        chosen, gate_columns = [], []
-        for j in range(held):
-            here = pick == (e % 8) * 2 + j
-            places = []
-            for u, slot_table in enumerate(slot_tables):
-                slot = jnp.sum(jnp.where(here, slot_table, 0.0), axis=0, keepdims=True)
-                places.append(jnp.where(slot >= 0, slot + float(u * cap), -1.0))
-            hot = target == jnp.concatenate(places, axis=1)
-            gate_line = jnp.concatenate(
-                [jnp.sum(jnp.where(here, t, 0.0), axis=0, keepdims=True) for t in gate_tables], axis=1
-            )
-            gate_columns.append(
-                jnp.sum(
-                    jnp.where(hot[2 * cap :, 2 * tokens :], gate_line, 0.0), axis=1, keepdims=True
-                )
-            )
-            chosen.append(
-                jnp.dot(
-                    jnp.where(hot, 1.0, 0.0).astype(jnp.bfloat16), x, preferred_element_type=jnp.float32
-                ).astype(jnp.bfloat16)
-            )
-        gate_rows[g] = jnp.broadcast_to(jnp.concatenate(gate_columns, axis=0), (held * 2 * cap, 128))
         for n in range(CHUNKS):
-            for side in range(2):
-                columns = slice(side * FF + n * chunk, side * FF + (n + 1) * chunk)
-                parts = [
-                    jnp.dot(chosen[j], weights[j, :, columns], preferred_element_type=jnp.float32)
-                    for j in range(held)
-                ]
-                here = slice(side * chunk, (side + 1) * chunk)
-                sent[g, n, :, here] = encode(
-                    jnp.concatenate([p[: 2 * cap] for p in parts], axis=0), scale
-                )
-                mine[g, n, :, here] = jnp.concatenate([p[2 * cap :] for p in parts], axis=0)
+            parts = [
+                jnp.dot(chosen[j], weights[n, j], preferred_element_type=jnp.float32)
+                for j in range(held)
+            ]
+            sent[g, n] = encode(jnp.concatenate([p[: 2 * cap] for p in parts], axis=0), scale)
             part_copy(g, n).start()
+            mine[g, n] = jnp.concatenate([p[2 * cap :] for p in parts], axis=0)
 
     def work(step, carry):
         zs, ys, other = chip_at_step(step, z, y)
         g = 2 * zs + ys
-        for i in range(2):
-            plane = c if i == 0 else 1 - c
-
-            @pl.when(step > 0)
-            def _():
-                unit_copy(g, k, plane, core_send.at[g * 2 + plane], core_peer).wait_recv()
-
-            if i == 1:
-
-                @pl.when(step == 0)
-                def _():
-                    x_rows(plane).wait_recv()
-                    x_table(plane).wait_recv()
-
-            each_send(step, plane, lambda copy: copy.start())
-        for i in range(2):
-            plane = c if i == 0 else 1 - c
-            unit_copy(g, 1 - k, plane, core_send.at[g * 2 + plane], core_peer).wait_recv()
+
+        @pl.when(step > 0)
+        def _():
+            unit_copy(g, k, c, core_send.at[g * 2 + c], core_peer).wait_recv()
+
+        each_send(step, c, lambda copy: copy.start())
+        unit_copy(g, 1 - k, c, core_send.at[g * 2 + c], core_peer).wait_recv()
+        ours = place(g, c, True)
 
         @pl.when(step == 0)
         def _():
             for w in weight_loads:
                 w.wait()
-
-        compute(g)
+            x_rows(1 - c).wait_recv()
+            x_table(1 - c).wait_recv()
+
+        @pl.when(step > 0)
+        def _():
+            unit_copy(g, k, 1 - c, core_send.at[g * 2 + 1 - c], core_peer).wait_recv()
+
+        each_send(step, 1 - c, lambda copy: copy.start())
+        unit_copy(g, 1 - k, 1 - c, core_send.at[g * 2 + 1 - c], core_peer).wait_recv()
+        compute(g, place(g, 1 - c, False), ours)
         return carry
 
     lax.fori_loop(0, CHIPS, work, 0)
@@ -307,6 +313,8 @@
         zs, ys, _ = chip_at_step(step, z, y)
         g = 2 * zs + ys
         gate_column = gate_rows[g, :, 0:1]
+        for plane in (c, 1 - c):
+            each_send(step, plane, lambda copy: copy.wait_send())
         for n in range(CHUNKS):
             part_copy(g, n).wait_recv()
             first = mine[g, n, :, :chunk] + decode(got[g, n, :, :chunk], scale)
@@ -318,21 +326,12 @@
                     out_ref[0, j, 2 * g + core, :, n * chunk : (n + 1) * chunk] = hidden[
                         low : low + cap
                     ].astype(jnp.bfloat16)
+            part_copy(g, n).wait_send()
         return carry
 
-    lax.fori_loop(0, CHIPS, finish, 0)
-
-    def drain(step, carry):
-        zs, ys, _ = chip_at_step(step, z, y)
-        for plane in (c, 1 - c):
-            each_send(step, plane, lambda copy: copy.wait_send())
-        for n in range(CHUNKS):
-            part_copy(2 * zs + ys, n).wait_send()
-        return carry
-
-    lax.fori_loop(0, CHIPS, drain, 0)
     x_rows(c).wait_send()
     x_table(c).wait_send()
+    lax.fori_loop(0, CHIPS, finish, 0)
 
 
 def kernel_shards(moe_rows, expert_ids, expert_gates, expert_weights):
@@ -352,13 +351,13 @@
         out_specs=vmem,
         scratch_shapes=[
             pltpu.VMEM((CHIPS, 2, 2, tokens + META, half), jnp.bfloat16),
-            pltpu.VMEM((held, half, columns), jnp.bfloat16),
+            pltpu.VMEM((CHUNKS, held, half, columns // CHUNKS), jnp.bfloat16),
             pltpu.VMEM((CHIPS, CHUNKS, part_rows, columns // CHUNKS), jnp.float32),
             pltpu.VMEM((CHIPS, CHUNKS, part_rows, columns // CHUNKS), jnp.bfloat16),
             pltpu.VMEM((CHIPS, CHUNKS, part_rows, columns // CHUNKS), jnp.bfloat16),
             pltpu.VMEM((CHIPS, part_rows, 128), jnp.float32),
             dma,
-            dma((held,)),
+            dma((CHUNKS * held * 2,)),
             dma((2,)),
             dma((2,)),
             dma((2 * ZS,)),

time: 94 us -> 96.8 us (1.030)
  Pallas kernels: 92.2 us -> 95.1 us
    pallas_call x1, Pallas kernels: 92.2 us -> 95.1 us  [kernel_shards(): pl.pallas_call(functools.partial(kernel, cap, scale), out_shape=pltpu.VME...]
where the time goes in v3:
time: 96.8 us; the launch traced here: 96.6 us
  Pallas kernels  95.1 us (98%)
  local copies, waits for them, and re-layouts  1.53 us (2%)
    pallas_call x1, Pallas kernels, kernel_shards(): pl.pallas_call(functools.partial(kernel, cap, scale), out_shape=pltpu.VME...  95.1 us

profile of v3, /device:TPU:0, one launch (start us, length us, event | category | flops | bytes accessed | tf_op | source)
XLA Modules:
  0.0 96.6 jit_solution(13333878403420319072)
XLA Ops:
  0.0 95.1 %shard_map.46 = bf16[1,2,16,36,768]{4,3,2,1,0:T(8,128)(2,1)S(1)} custom-call(bf16[128,2048]{1,0:T(8,128)(2,1)} %rows_ref.1, s32[8,128]{1,0:T(8,128)} %bitcast.2, bf16[8,128]{1,0:T(8,128)(2,1)} %bitcast.3, bf16[2,1024,1536]{2,1,0:T(8,128)(2,1)} %weights_hbm.1), custom_call_target="tpu_custom_call" | custom-call | flops 7247757312 | bytes 6291456 | tf_op jit(solution)/shard_map/pallas_call | solution.py:347
  95.1 1.5 %copy.5 = bf16[1,2,16,36,768]{4,2,3,1,0:T(8,128)(2,1)} copy(bf16[1,2,16,36,768]{4,3,2,1,0:T(8,128)(2,1)S(1)} %shard_map.46) | data formatting | bytes 3538944 | tf_op jit(solution)/shard_map/pallas_call | solution.py:347

commit v4 on v3

--- a/solution.py
+++ b/solution.py
@@ -15,7 +15,7 @@
 META = 16
 ZS = 4
 CHIPS = 8
-CHUNKS = 6
+CHUNKS = 3
 
 
 def place_rows(block_rows, block_ids, block_gates, experts, capacity):
@@ -139,17 +139,8 @@
     )
     load.start()
     weight_loads = [
-        pltpu.make_async_copy(
-            weights_hbm.at[j, :, pl.ds(side * FF + n * chunk, chunk)],
-            weights.at[n, j, :, pl.ds(side * chunk, chunk)],
-            weight_sem.at[(n * held + j) * 2 + side],
-        )
-        for n in range(CHUNKS)
-        for j in range(held)
-        for side in range(2)
+        pltpu.make_async_copy(weights_hbm.at[j], weights.at[j], weight_sem.at[j]) for j in range(held)
     ]
-    for w in weight_loads:
-        w.start()
 
     expert = lax.broadcasted_iota(jnp.int32, (32, tokens), 0)
     ids = ids_ref[...]
@@ -201,6 +192,8 @@
 
     x_rows(c).start()
     x_table(c).start()
+    for w in weight_loads:
+        w.start()
     load.wait()
 
     def unit_copy(g, core, plane, send_sem, peer):
@@ -271,13 +264,18 @@
             jnp.concatenate([theirs[r], ours[r]], axis=0).astype(jnp.bfloat16) for r in rows
         ]
         for n in range(CHUNKS):
-            parts = [
-                jnp.dot(chosen[j], weights[n, j], preferred_element_type=jnp.float32)
-                for j in range(held)
-            ]
-            sent[g, n] = encode(jnp.concatenate([p[: 2 * cap] for p in parts], axis=0), scale)
+            for side in range(2):
+                columns = slice(side * FF + n * chunk, side * FF + (n + 1) * chunk)
+                here = slice(side * chunk, (side + 1) * chunk)
+                parts = [
+                    jnp.dot(chosen[j], weights[j, :, columns], preferred_element_type=jnp.float32)
+                    for j in range(held)
+                ]
+                sent[g, n, :, here] = encode(
+                    jnp.concatenate([p[: 2 * cap] for p in parts], axis=0), scale
+                )
+                mine[g, n, :, here] = jnp.concatenate([p[2 * cap :] for p in parts], axis=0)
             part_copy(g, n).start()
-            mine[g, n] = jnp.concatenate([p[2 * cap :] for p in parts], axis=0)
 
     def work(step, carry):
         zs, ys, other = chip_at_step(step, z, y)
@@ -351,13 +349,13 @@
         out_specs=vmem,
         scratch_shapes=[
             pltpu.VMEM((CHIPS, 2, 2, tokens + META, half), jnp.bfloat16),
-            pltpu.VMEM((CHUNKS, held, half, columns // CHUNKS), jnp.bfloat16),
+            pltpu.VMEM((held, half, columns), jnp.bfloat16),
             pltpu.VMEM((CHIPS, CHUNKS, part_rows, columns // CHUNKS), jnp.float32),
             pltpu.VMEM((CHIPS, CHUNKS, part_rows, columns // CHUNKS), jnp.bfloat16),
             pltpu.VMEM((CHIPS, CHUNKS, part_rows, columns // CHUNKS), jnp.bfloat16),
             pltpu.VMEM((CHIPS, part_rows, 128), jnp.float32),
             dma,
-            dma((CHUNKS * held * 2,)),
+            dma((held,)),
             dma((2,)),
             dma((2,)),
             dma((2 * ZS,)),

time: 96.8 us -> 93.8 us (0.969)
  Pallas kernels: 95.1 us -> 92.1 us
    pallas_call x1, Pallas kernels: 95.1 us -> 92.1 us  [kernel_shards(): pl.pallas_call(functools.partial(kernel, cap, scale), out_shape=pltpu.VME...]
where the time goes in v4:
time: 93.8 us; the launch traced here: 93.6 us
  Pallas kernels  92.1 us (98%)
  local copies, waits for them, and re-layouts  1.53 us (2%)
    pallas_call x1, Pallas kernels, kernel_shards(): pl.pallas_call(functools.partial(kernel, cap, scale), out_shape=pltpu.VME...  92.1 us

profile of v4, /device:TPU:0, one launch (start us, length us, event | category | flops | bytes accessed | tf_op | source)
XLA Modules:
  0.0 93.6 jit_solution(901951210506660756)
XLA Ops:
  0.0 92.1 %shard_map.46 = bf16[1,2,16,36,768]{4,3,2,1,0:T(8,128)(2,1)S(1)} custom-call(bf16[128,2048]{1,0:T(8,128)(2,1)} %rows_ref.1, s32[8,128]{1,0:T(8,128)} %bitcast.2, bf16[8,128]{1,0:T(8,128)(2,1)} %bitcast.3, bf16[2,1024,1536]{2,1,0:T(8,128)(2,1)} %weights_hbm.1), custom_call_target="tpu_custom_call" | custom-call | flops 7247757312 | bytes 6291456 | tf_op jit(solution)/shard_map/pallas_call | solution.py:345
  92.1 1.5 %copy.5 = bf16[1,2,16,36,768]{4,2,3,1,0:T(8,128)(2,1)} copy(bf16[1,2,16,36,768]{4,3,2,1,0:T(8,128)(2,1)S(1)} %shard_map.46) | data formatting | bytes 3538944 | tf_op jit(solution)/shard_map/pallas_call | solution.py:345

commit v5 on v4

--- a/solution.py
+++ b/solution.py
@@ -277,35 +277,46 @@
                 mine[g, n, :, here] = jnp.concatenate([p[2 * cap :] for p in parts], axis=0)
             part_copy(g, n).start()
 
+    def chip_of(step):
+        zs, ys, _ = chip_at_step(step, z, y)
+        return 2 * zs + ys
+
+    def from_core(g, plane):
+        unit_copy(g, 1 - k, plane, core_send.at[g * 2 + plane], core_peer).wait_recv()
+
+    def forward(step):
+        g = chip_of(step)
+        for plane in (c, 1 - c):
+            unit_copy(g, k, plane, core_send.at[g * 2 + plane], core_peer).wait_recv()
+            each_send(step, plane, lambda copy: copy.start())
+
     def work(step, carry):
-        zs, ys, other = chip_at_step(step, z, y)
-        g = 2 * zs + ys
-
-        @pl.when(step > 0)
+        @pl.when(step % 2 == 1)
         def _():
-            unit_copy(g, k, c, core_send.at[g * 2 + c], core_peer).wait_recv()
-
-        each_send(step, c, lambda copy: copy.start())
-        unit_copy(g, 1 - k, c, core_send.at[g * 2 + c], core_peer).wait_recv()
+            forward(step)
+
+            @pl.when(step < CHIPS - 1)
+            def _():
+                forward(step + 1)
+
+        g = chip_of(step)
+        from_core(g, c)
+        from_core(g, 1 - c)
         ours = place(g, c, True)
-
-        @pl.when(step == 0)
-        def _():
-            for w in weight_loads:
-                w.wait()
-            x_rows(1 - c).wait_recv()
-            x_table(1 - c).wait_recv()
-
-        @pl.when(step > 0)
-        def _():
-            unit_copy(g, k, 1 - c, core_send.at[g * 2 + 1 - c], core_peer).wait_recv()
-
-        each_send(step, 1 - c, lambda copy: copy.start())
-        unit_copy(g, 1 - k, 1 - c, core_send.at[g * 2 + 1 - c], core_peer).wait_recv()
         compute(g, place(g, 1 - c, False), ours)
         return carry
 
-    lax.fori_loop(0, CHIPS, work, 0)
+    each_send(0, c, lambda copy: copy.start())
+    from_core(chip, c)
+    ours = place(chip, c, True)
+    for w in weight_loads:
+        w.wait()
+    x_rows(1 - c).wait_recv()
+    x_table(1 - c).wait_recv()
+    each_send(0, 1 - c, lambda copy: copy.start())
+    from_core(chip, 1 - c)
+    compute(chip, place(chip, 1 - c, False), ours)
+    lax.fori_loop(1, CHIPS, work, 0)
 
     def finish(step, carry):
         zs, ys, _ = chip_at_step(step, z, y)

time: 93.8 us -> 93 us (level)
  no operation moved by 1% of the time
where the time goes in v5:
time: 93 us; the launch traced here: 92.8 us
  Pallas kernels  91.3 us (98%)
  local copies, waits for them, and re-layouts  1.53 us (2%)
    pallas_call x1, Pallas kernels, kernel_shards(): pl.pallas_call(functools.partial(kernel, cap, scale), out_shape=pltpu.VME...  91.3 us

profile of v5, /device:TPU:0, one launch (start us, length us, event | category | flops | bytes accessed | tf_op | source)
XLA Modules:
  0.0 92.8 jit_solution(1655998394383080873)
XLA Ops:
  0.0 91.3 %shard_map.46 = bf16[1,2,16,36,768]{4,3,2,1,0:T(8,128)(2,1)S(1)} custom-call(bf16[128,2048]{1,0:T(8,128)(2,1)} %rows_ref.1, s32[8,128]{1,0:T(8,128)} %bitcast.2, bf16[8,128]{1,0:T(8,128)(2,1)} %bitcast.3, bf16[2,1024,1536]{2,1,0:T(8,128)(2,1)} %weights_hbm.1), custom_call_target="tpu_custom_call" | custom-call | flops 7247757312 | bytes 6291456 | tf_op jit(solution)/shard_map/pallas_call | solution.py:356
  91.3 1.5 %copy.5 = bf16[1,2,16,36,768]{4,2,3,1,0:T(8,128)(2,1)} copy(bf16[1,2,16,36,768]{4,3,2,1,0:T(8,128)(2,1)S(1)} %shard_map.46) | data formatting | bytes 3538944 | tf_op jit(solution)/shard_map/pallas_call | solution.py:356

commit v6 on v5

--- a/solution.py
+++ b/solution.py
@@ -95,9 +95,9 @@
 
 def kernel(
     cap, scale,
-    rows_ref, ids_ref, gates_ref, weights_hbm, out_ref,
+    rows_ref, ids_hbm, gates_hbm, weights_hbm, out_ref,
     blocks, weights, mine, sent, got, gate_rows,
-    load_sem, weight_sem, x_send, x_recv, up_send, down_send, y_send, core_send, unit_recv,
+    ids_ref, gates_ref, load_sem, small_sem, weight_sem, x_send, x_recv, up_send, down_send, y_send, core_send, unit_recv,
     part_send, part_recv,
 ):
     tokens, width = rows_ref.shape
@@ -137,10 +137,42 @@
         blocks.at[chip, k, c, pl.ds(0, tokens)],
         load_sem,
     )
+    small_loads = [
+        pltpu.make_async_copy(ids_hbm, ids_ref, small_sem.at[0]),
+        pltpu.make_async_copy(gates_hbm, gates_ref, small_sem.at[1]),
+    ]
+    for copy in small_loads:
+        copy.start()
     load.start()
     weight_loads = [
         pltpu.make_async_copy(weights_hbm.at[j], weights.at[j], weight_sem.at[j]) for j in range(held)
     ]
+
+    pl.semaphore_wait(barrier, 3 + (z + ZS - 1) // ZS + (2 * ZS - 2 - z) // ZS)
+
+    def remote(src, dst, send_sem, recv_sem, peer):
+        return pltpu.make_async_remote_copy(
+            src_ref=src, dst_ref=dst, send_sem=send_sem, recv_sem=recv_sem,
+            device_id=peer, device_id_type=pl.DeviceIdType.MESH,
+        )
+
+    def x_rows(plane):
+        return remote(
+            rows_ref.at[:, pl.ds(pl.multiple_of((1 - c) * half, half), half)],
+            blocks.at[chip, k, plane, pl.ds(0, tokens)],
+            x_send.at[0], x_recv.at[0], x_peer,
+        )
+
+    def x_table(plane):
+        return remote(
+            blocks.at[chip, k, plane, pl.ds(tokens, META), pl.ds(0, 512)],
+            blocks.at[chip, k, plane, pl.ds(tokens, META), pl.ds(0, 512)],
+            x_send.at[1], x_recv.at[1], x_peer,
+        )
+
+    x_rows(c).start()
+    for copy in small_loads:
+        copy.wait()
 
     expert = lax.broadcasted_iota(jnp.int32, (32, tokens), 0)
     ids = ids_ref[...]
@@ -168,29 +200,6 @@
     blocks[chip, k, c, tokens:, :] = table.astype(jnp.bfloat16)
     blocks[chip, k, 1 - c, tokens:, 512:] = jnp.zeros((META, half - 512), jnp.bfloat16)
 
-    pl.semaphore_wait(barrier, 3 + (z + ZS - 1) // ZS + (2 * ZS - 2 - z) // ZS)
-
-    def remote(src, dst, send_sem, recv_sem, peer):
-        return pltpu.make_async_remote_copy(
-            src_ref=src, dst_ref=dst, send_sem=send_sem, recv_sem=recv_sem,
-            device_id=peer, device_id_type=pl.DeviceIdType.MESH,
-        )
-
-    def x_rows(plane):
-        return remote(
-            rows_ref.at[:, pl.ds(pl.multiple_of((1 - c) * half, half), half)],
-            blocks.at[chip, k, plane, pl.ds(0, tokens)],
-            x_send.at[0], x_recv.at[0], x_peer,
-        )
-
-    def x_table(plane):
-        return remote(
-            blocks.at[chip, k, plane, pl.ds(tokens, META), pl.ds(0, 512)],
-            blocks.at[chip, k, plane, pl.ds(tokens, META), pl.ds(0, 512)],
-            x_send.at[1], x_recv.at[1], x_peer,
-        )
-
-    x_rows(c).start()
     x_table(c).start()
     for w in weight_loads:
         w.start()
@@ -356,7 +365,7 @@
     return pl.pallas_call(
         functools.partial(kernel, cap, scale),
         out_shape=pltpu.VMEM((1, held, sources, cap, columns // 2), jnp.bfloat16),
-        in_specs=[hbm, vmem, vmem, hbm],
+        in_specs=[hbm, hbm, hbm, hbm],
         out_specs=vmem,
         scratch_shapes=[
             pltpu.VMEM((CHIPS, 2, 2, tokens + META, half), jnp.bfloat16),
@@ -365,7 +374,10 @@
             pltpu.VMEM((CHIPS, CHUNKS, part_rows, columns // CHUNKS), jnp.bfloat16),
             pltpu.VMEM((CHIPS, CHUNKS, part_rows, columns // CHUNKS), jnp.bfloat16),
             pltpu.VMEM((CHIPS, part_rows, 128), jnp.float32),
+            pltpu.VMEM((TOP, tokens), jnp.int32),
+            pltpu.VMEM((TOP, tokens), jnp.bfloat16),
             dma,
+            dma((2,)),
             dma((held,)),
             dma((2,)),
             dma((2,)),

time: 93 us -> 92.3 us (level)
  no operation moved by 1% of the time
where the time goes in v6:
time: 92.3 us; the launch traced here: 92.2 us
  Pallas kernels  90.6 us (98%)
  local copies, waits for them, and re-layouts  1.53 us (2%)
    pallas_call x1, Pallas kernels, kernel_shards(): pl.pallas_call(functools.partial(kernel, cap, scale), out_shape=pltpu.VME...  90.6 us

profile of v6, /device:TPU:0, one launch (start us, length us, event | category | flops | bytes accessed | tf_op | source)
XLA Modules:
  0.0 92.2 jit_solution(4994067346594548933)
XLA Ops:
  0.0 90.6 %shard_map.46 = bf16[1,2,16,36,768]{4,3,2,1,0:T(8,128)(2,1)S(1)} custom-call(bf16[128,2048]{1,0:T(8,128)(2,1)} %rows_ref.1, s32[8,128]{1,0:T(8,128)} %bitcast.2, bf16[8,128]{1,0:T(8,128)(2,1)} %bitcast.3, bf16[2,1024,1536]{2,1,0:T(8,128)(2,1)} %weights_hbm.1), custom_call_target="tpu_custom_call" | custom-call | flops 7247757312 | bytes 6291456 | tf_op jit(solution)/shard_map/pallas_call | solution.py:365
  90.6 1.5 %copy.5 = bf16[1,2,16,36,768]{4,2,3,1,0:T(8,128)(2,1)} copy(bf16[1,2,16,36,768]{4,3,2,1,0:T(8,128)(2,1)S(1)} %shard_map.46) | data formatting | bytes 3538944 | tf_op jit(solution)/shard_map/pallas_call | solution.py:365

commit v7 on v6

--- a/solution.py
+++ b/solution.py
@@ -273,6 +273,7 @@
             jnp.concatenate([theirs[r], ours[r]], axis=0).astype(jnp.bfloat16) for r in rows
         ]
         for n in range(CHUNKS):
+            kept = []
             for side in range(2):
                 columns = slice(side * FF + n * chunk, side * FF + (n + 1) * chunk)
                 here = slice(side * chunk, (side + 1) * chunk)
@@ -283,8 +284,10 @@
                 sent[g, n, :, here] = encode(
                     jnp.concatenate([p[: 2 * cap] for p in parts], axis=0), scale
                 )
-                mine[g, n, :, here] = jnp.concatenate([p[2 * cap :] for p in parts], axis=0)
+                kept.append((here, jnp.concatenate([p[2 * cap :] for p in parts], axis=0)))
             part_copy(g, n).start()
+            for here, value in kept:
+                mine[g, n, :, here] = value
 
     def chip_of(step):
         zs, ys, _ = chip_at_step(step, z, y)

time: 92.3 us -> 92.3 us (level)
  no operation moved by 1% of the time
where the time goes in v7:
time: 92.3 us; the launch traced here: 92.1 us
  Pallas kernels  90.6 us (98%)
  local copies, waits for them, and re-layouts  1.53 us (2%)
    pallas_call x1, Pallas kernels, kernel_shards(): pl.pallas_call(functools.partial(kernel, cap, scale), out_shape=pltpu.VME...  90.6 us

profile of v7, /device:TPU:0, one launch (start us, length us, event | category | flops | bytes accessed | tf_op | source)
XLA Modules:
  0.0 92.1 jit_solution(13551206637687391965)
XLA Ops:
  0.0 90.6 %shard_map.46 = bf16[1,2,16,36,768]{4,3,2,1,0:T(8,128)(2,1)S(1)} custom-call(bf16[128,2048]{1,0:T(8,128)(2,1)} %rows_ref.1, s32[8,128]{1,0:T(8,128)} %bitcast.2, bf16[8,128]{1,0:T(8,128)(2,1)} %bitcast.3, bf16[2,1024,1536]{2,1,0:T(8,128)(2,1)} %weights_hbm.1), custom_call_target="tpu_custom_call" | custom-call | flops 7247757312 | bytes 6291456 | tf_op jit(solution)/shard_map/pallas_call | solution.py:368
  90.6 1.5 %copy.5 = bf16[1,2,16,36,768]{4,2,3,1,0:T(8,128)(2,1)} copy(bf16[1,2,16,36,768]{4,3,2,1,0:T(8,128)(2,1)S(1)} %shard_map.46) | data formatting | bytes 3538944 | tf_op jit(solution)/shard_map/pallas_call | solution.py:368
